TPU v7x, 32 devices: a whole 2x2x4 slice. The times are simulated.
32 devices in a mesh: row: 2 (over core), seq: 16 (over z, y, x).
Axes of the slice: x: 2, y: 2, z: 4, core: 2. Of those that a mesh axis runs over, the one named last changes fastest.
Arguments:
- block_in: bfloat16 [4, 4096, 768], P('row', 'seq'), may hold values from -6 to 6
- lengths: int32 [4, 8], P('row'), may hold values from 1 to 3841, as said below
- mixer_gain: float32 [768], replicated, may hold values from 0.5 to 1.5
- mixer_bias: float32 [768], replicated, may hold values from -1.75 to 1.75
- in_weight: bfloat16 [768, 2304], replicated, may hold values from -0.21875 to 0.21875
- short_taps: float32 [3, 2304], replicated, may hold values from -4 to 4
- filter_in: float32 [33, 64], replicated, may hold values from -2 to 2
- filter_in_bias: float32 [64], replicated, may hold values from -3.140625 to 3.140625
- filter_mid: float32 [64, 64], replicated, may hold values from -1.5 to 1.5
- filter_mid_bias: float32 [64], replicated, may hold values from -3.140625 to 3.140625
- filter_freq: float32 [64], replicated, may hold values from 0.5 to 2
- filter_out: float32 [64, 768], replicated, may hold values from -0.03125 to 0.03125
- filter_skip: float32 [768], replicated, may hold values from -6 to 6
- decay_rate: float32 [768], replicated, may hold values from 1.2207031e-05 to 0.1
- out_weight: bfloat16 [768, 768], replicated, may hold values from -0.4375 to 0.4375
- feed_gain: float32 [768], replicated, may hold values from 0.5 to 1.5
- feed_bias: float32 [768], replicated, may hold values from -1.75 to 1.75
- up_weight: bfloat16 [768, 3072], replicated, may hold values from -0.21875 to 0.21875
- down_weight: bfloat16 [3072, 768], replicated, may hold values from -0.15625 to 0.15625
- cotangent: bfloat16 [4, 4096, 768], P('row', 'seq'), may hold values from -6 to 6
Outputs:
- block_out: bfloat16 [4, 4096, 768], P('row', 'seq')
- grad_input: float32 [4, 4096, 768], P('row', 'seq')
- grad_mixer_gain: float32 [768], replicated
- grad_mixer_bias: float32 [768], replicated
- grad_in_weight: float32 [768, 2304], P('seq')
- grad_short_taps: float32 [3, 2304], replicated
- grad_filter_in: float32 [33, 64], replicated
- grad_filter_in_bias: float32 [64], replicated
- grad_filter_mid: float32 [64, 64], replicated
- grad_filter_mid_bias: float32 [64], replicated
- grad_filter_freq: float32 [64], replicated
- grad_filter_out: float32 [64, 768], replicated
- grad_filter_skip: float32 [768], replicated
- grad_out_weight: float32 [768, 768], P('seq')
- grad_feed_gain: float32 [768], replicated
- grad_feed_bias: float32 [768], replicated
- grad_up_weight: float32 [768, 3072], P('seq')
- grad_down_weight: float32 [3072, 768], P('seq')
Inputs may be any that keep to these rules, and one draw needn't show every extreme that they name: `lengths`: lengths are positive; in each row they sum to less than 4096, and the positions after their sum are padding.
All inputs are finite; a program needn't handle non-finite values.
Results may differ from a plain program's by a relative error of at most 0.015.
Values may be sent and summed in bfloat16 or wider, within the bound.
A program may use at most 256 MiB of HBM per device.

v0:
```python
import math

import jax
import jax.numpy as jnp
from jax import lax
from jax.sharding import PartitionSpec as P

HIGHEST = lax.Precision.HIGHEST


def shifted(array, axis, by):
    peers = lax.axis_size(axis)
    pairs = [(i, i + by) for i in range(peers) if 0 <= i + by < peers]
    return lax.ppermute(array, axis, pairs)


def layer_norm(values, gain, offset):
    center = values - jnp.mean(values, axis=-1, keepdims=True)
    spread = jnp.mean(center * center, axis=-1, keepdims=True)
    return center * lax.rsqrt(spread + 1e-05) * gain + offset


def features(length, feat_count):
    band_count = (feat_count - 1) // 2
    positions = jnp.arange(length, dtype=jnp.int32)
    band_freq = jnp.arange(1, band_count + 1, dtype=jnp.int32)
    turn_index = positions[:, None] * band_freq[None, :] % length
    angles = 2.0 * math.pi / length * turn_index.astype(jnp.float32)
    ramp_feat = positions.astype(jnp.float32)[:, None] / length
    return jnp.concatenate([ramp_feat, jnp.cos(angles), -jnp.sin(angles)], axis=1)


def filter_rows(
    filter_in,
    filter_in_bias,
    filter_mid,
    filter_mid_bias,
    filter_freq,
    out_part,
    decay_part,
    length,
):
    feats = features(length, filter_in.shape[0])
    hidden = jnp.sin(filter_freq * (jnp.dot(feats, filter_in, precision=HIGHEST) + filter_in_bias))
    hidden = jnp.sin(
        filter_freq * (jnp.dot(hidden, filter_mid, precision=HIGHEST) + filter_mid_bias)
    )
    raw_filter = jnp.einsum("lh,hc->cl", hidden, out_part, precision=HIGHEST)
    positions = jnp.arange(length, dtype=jnp.float32)
    return raw_filter * jnp.exp(-decay_part[:, None] * positions[None, :])


def angle_table(angle_index, period):
    turned = 2.0 * math.pi / period * angle_index.astype(jnp.float32)
    return (jnp.cos(turned), jnp.sin(turned))


def dft_tables(length):
    half_rows = math.isqrt(length // 2)
    while length % half_rows:
        half_rows = half_rows - 1
    full_rows = 2 * half_rows
    col_count = length // half_rows
    total = full_rows * col_count
    row_index = jnp.arange(full_rows, dtype=jnp.int32)
    col_index = jnp.arange(col_count, dtype=jnp.int32)
    first_table = angle_table(
        row_index[:, None] * row_index[None, :half_rows] % full_rows, full_rows
    )
    second = angle_table(col_index[:, None] * col_index[None, :] % col_count, col_count)
    twiddle = angle_table(row_index[:, None] * col_index[None, :] % total, total)
    return (half_rows, col_count, first_table, second, twiddle)


def forward_dft(signal, tables):
    half_rows, col_count, first_table, second, twiddle = tables
    leading = signal.shape[:-1]
    grid_view = signal.reshape(leading + (half_rows, col_count))
    real_part = jnp.einsum("kn,...nm->...km", first_table[0], grid_view, precision=HIGHEST)
    imag_part = -jnp.einsum("kn,...nm->...km", first_table[1], grid_view, precision=HIGHEST)
    turn_real = real_part * twiddle[0] + imag_part * twiddle[1]
    turn_imag = imag_part * twiddle[0] - real_part * twiddle[1]
    out_real = jnp.einsum("...kn,nj->...kj", turn_real, second[0], precision=HIGHEST) + jnp.einsum(
        "...kn,nj->...kj", turn_imag, second[1], precision=HIGHEST
    )
    out_imag = jnp.einsum("...kn,nj->...kj", turn_imag, second[0], precision=HIGHEST) - jnp.einsum(
        "...kn,nj->...kj", turn_real, second[1], precision=HIGHEST
    )
    return (out_real, out_imag)


def inverse_dft(spec_real, spec_imag, tables):
    half_rows, col_count, first_table, second, twiddle = tables
    leading = spec_real.shape[:-2]
    real_part = jnp.einsum("...kj,jn->...kn", spec_real, second[0], precision=HIGHEST) - jnp.einsum(
        "...kj,jn->...kn", spec_imag, second[1], precision=HIGHEST
    )
    imag_part = jnp.einsum("...kj,jn->...kn", spec_imag, second[0], precision=HIGHEST) + jnp.einsum(
        "...kj,jn->...kn", spec_real, second[1], precision=HIGHEST
    )
    turn_real = real_part * twiddle[0] - imag_part * twiddle[1]
    turn_imag = imag_part * twiddle[0] + real_part * twiddle[1]
    grid_view = jnp.einsum(
        "kn,...km->...nm", first_table[0], turn_real, precision=HIGHEST
    ) - jnp.einsum("kn,...km->...nm", first_table[1], turn_imag, precision=HIGHEST)
    grid_view = grid_view * (1.0 / (2 * half_rows * col_count))
    return grid_view.reshape(leading + (half_rows * col_count,))


def shards(
    block_in,
    lengths,
    mixer_gain,
    mixer_bias,
    in_weight,
    short_taps,
    filter_in,
    filter_in_bias,
    filter_mid,
    filter_mid_bias,
    filter_freq,
    filter_out,
    filter_skip,
    decay_rate,
    out_weight,
    feed_gain,
    feed_bias,
    up_weight,
    down_weight,
    cotangent,
):
    row_count, tok_count, model_width = block_in.shape
    groups = lax.axis_size("seq")
    length = tok_count * groups
    narrow = model_width // groups
    seq_place = lax.axis_index("seq")
    chan_start = seq_place * narrow
    positions = seq_place * tok_count + jnp.arange(tok_count, dtype=jnp.int32)
    doc_ends = jnp.cumsum(lengths, axis=1)
    live_mask = (positions[None, :] < doc_ends[:, -1:]).astype(jnp.float32)

    def doc_of(where):
        return jnp.sum((where[None, :, None] >= doc_ends[:, None, :]).astype(jnp.int32), axis=2)

    own_doc = doc_of(positions)
    tap_masks = []
    for tap_lag in range(3):
        same_doc = (positions[None, :] >= tap_lag) & (doc_of(positions - tap_lag) == own_doc)
        tap_masks.append(same_doc.astype(jnp.float32))
    block_float = block_in.astype(jnp.float32)
    normed, norm_pull = jax.vjp(layer_norm, block_float, mixer_gain, mixer_bias)
    normed_low = normed.astype(jnp.bfloat16)
    projected = jnp.einsum(
        "rtd,dc->rct", normed_low, in_weight, preferred_element_type=jnp.float32
    ).astype(jnp.bfloat16)
    left_rim = shifted(projected[:, :, tok_count - 2 :], "seq", 1)
    extended = jnp.concatenate([left_rim, projected], axis=2).astype(jnp.float32)
    short_mix = jnp.zeros(projected.shape, jnp.float32)
    for tap_lag in range(3):
        window = extended[:, :, 2 - tap_lag : 2 - tap_lag + tok_count]
        short_mix = (
            short_mix + short_taps[tap_lag][None, :, None] * window * tap_masks[tap_lag][:, None, :]
        )
    gate_out = short_mix[:, :model_width]
    gate_in = short_mix[:, model_width : 2 * model_width]
    stream_v = short_mix[:, 2 * model_width :]
    carried = (gate_in * stream_v * live_mask[:, None, :]).astype(jnp.bfloat16)
    spread_in = lax.all_to_all(carried, "seq", split_axis=1, concat_axis=2, tiled=True)
    out_part = lax.dynamic_slice_in_dim(filter_out, chan_start, narrow, 1)
    decay_part = lax.dynamic_slice_in_dim(decay_rate, chan_start, narrow, 0)
    skip_part = lax.dynamic_slice_in_dim(filter_skip, chan_start, narrow, 0)

    def build_filter(first_w, first_b, mid_w, mid_b, freq_w, last_w):
        return filter_rows(first_w, first_b, mid_w, mid_b, freq_w, last_w, decay_part, length)

    filt, filter_pull = jax.vjp(
        build_filter, filter_in, filter_in_bias, filter_mid, filter_mid_bias, filter_freq, out_part
    )
    tables = dft_tables(length)
    signal = spread_in.astype(jnp.float32)
    sig_real, sig_imag = forward_dft(signal, tables)
    fil_real, fil_imag = forward_dft(filt, tables)
    conv = inverse_dft(
        sig_real * fil_real - sig_imag * fil_imag, sig_real * fil_imag + sig_imag * fil_real, tables
    )
    conv = conv + skip_part[None, :, None] * signal
    back_home = lax.all_to_all(
        conv.astype(jnp.bfloat16), "seq", split_axis=2, concat_axis=1, tiled=True
    )
    conv_float = back_home.astype(jnp.float32)
    product_low = (gate_out * conv_float * live_mask[:, None, :]).astype(jnp.bfloat16)
    mixed = block_float + jnp.einsum(
        "rct,cd->rtd", product_low, out_weight, preferred_element_type=jnp.float32
    )
    normed_two, feed_pull = jax.vjp(layer_norm, mixed, feed_gain, feed_bias)
    normed_two_low = normed_two.astype(jnp.bfloat16)
    pre_act = jnp.einsum(
        "rtd,df->rtf", normed_two_low, up_weight, preferred_element_type=jnp.float32
    )
    activ, gelu_pull = jax.vjp(jax.nn.gelu, pre_act)
    activ_low = activ.astype(jnp.bfloat16)
    block_out = (
        mixed
        + jnp.einsum("rtf,fd->rtd", activ_low, down_weight, preferred_element_type=jnp.float32)
    ).astype(jnp.bfloat16)
    grad_float = cotangent.astype(jnp.float32)
    grad_down = jnp.einsum("rtf,rtd->fd", activ_low, cotangent, preferred_element_type=jnp.float32)
    grad_activ = jnp.einsum(
        "rtd,fd->rtf", cotangent, down_weight, preferred_element_type=jnp.float32
    )
    grad_pre = gelu_pull(grad_activ)[0].astype(jnp.bfloat16)
    grad_up = jnp.einsum(
        "rtd,rtf->df", normed_two_low, grad_pre, preferred_element_type=jnp.float32
    )
    grad_normed_two = jnp.einsum(
        "rtf,df->rtd", grad_pre, up_weight, preferred_element_type=jnp.float32
    )
    grad_mixed_part, grad_feed_gain, grad_feed_bias = feed_pull(grad_normed_two)
    grad_mixed = grad_float + grad_mixed_part
    grad_mixed_low = grad_mixed.astype(jnp.bfloat16)
    grad_outw = jnp.einsum(
        "rct,rtd->cd", product_low, grad_mixed_low, preferred_element_type=jnp.float32
    )
    grad_product = (
        jnp.einsum("rtd,cd->rct", grad_mixed_low, out_weight, preferred_element_type=jnp.float32)
        * live_mask[:, None, :]
    )
    grad_gate_out = grad_product * conv_float
    grad_conv = (grad_product * gate_out).astype(jnp.bfloat16)
    grad_spread = lax.all_to_all(grad_conv, "seq", split_axis=1, concat_axis=2, tiled=True).astype(
        jnp.float32
    )
    back_real, back_imag = forward_dft(grad_spread, tables)
    grad_signal = inverse_dft(
        fil_real * back_real + fil_imag * back_imag,
        fil_real * back_imag - fil_imag * back_real,
        tables,
    )
    grad_signal = grad_signal + skip_part[None, :, None] * grad_spread
    grad_filt = inverse_dft(
        jnp.sum(sig_real * back_real + sig_imag * back_imag, axis=0),
        jnp.sum(sig_real * back_imag - sig_imag * back_real, axis=0),
        tables,
    )
    grad_skip_part = jnp.sum(grad_spread * signal, axis=(0, 2))
    grad_first_w, grad_first_b, grad_mid_w, grad_mid_b, grad_freq_w, grad_last_part = filter_pull(
        grad_filt
    )
    grad_carried = lax.all_to_all(
        grad_signal.astype(jnp.bfloat16), "seq", split_axis=2, concat_axis=1, tiled=True
    )
    grad_carried = grad_carried.astype(jnp.float32) * live_mask[:, None, :]
    grad_short = jnp.concatenate(
        [grad_gate_out, grad_carried * stream_v, grad_carried * gate_in], axis=1
    )
    grad_extended = jnp.zeros(extended.shape, jnp.float32)
    tap_grads = []
    for tap_lag in range(3):
        masked = grad_short * tap_masks[tap_lag][:, None, :]
        window = extended[:, :, 2 - tap_lag : 2 - tap_lag + tok_count]
        tap_grads.append(jnp.sum(masked * window, axis=(0, 2)))
        grad_extended = grad_extended + jnp.pad(
            short_taps[tap_lag][None, :, None] * masked, ((0, 0), (0, 0), (2 - tap_lag, tap_lag))
        )
    grad_taps = jnp.stack(tap_grads)
    rim_back = shifted(grad_extended[:, :, :2].astype(jnp.bfloat16), "seq", -1).astype(jnp.float32)
    grad_proj = grad_extended[:, :, 2:] + jnp.pad(rim_back, ((0, 0), (0, 0), (tok_count - 2, 0)))
    grad_proj_low = grad_proj.astype(jnp.bfloat16)
    grad_inw = jnp.einsum(
        "rtd,rct->dc", normed_low, grad_proj_low, preferred_element_type=jnp.float32
    )
    grad_normed = jnp.einsum(
        "rct,dc->rtd", grad_proj_low, in_weight, preferred_element_type=jnp.float32
    )
    grad_input_part, grad_mixer_gain, grad_mixer_bias = norm_pull(grad_normed)
    grad_input = grad_mixed + grad_input_part
    grad_last = lax.dynamic_update_slice_in_dim(
        jnp.zeros(filter_out.shape, jnp.float32), grad_last_part, chan_start, 1
    )
    grad_skip = lax.dynamic_update_slice_in_dim(
        jnp.zeros(filter_skip.shape, jnp.float32), grad_skip_part, chan_start, 0
    )
    summed = lax.psum(
        (
            grad_mixer_gain,
            grad_mixer_bias,
            grad_taps,
            grad_first_w,
            grad_first_b,
            grad_mid_w,
            grad_mid_b,
            grad_freq_w,
            grad_last,
            grad_skip,
            grad_feed_gain,
            grad_feed_bias,
        ),
        ("row", "seq"),
    )
    shares = (
        lax.psum_scatter(
            grad_inw.astype(jnp.bfloat16), "seq", scatter_dimension=0, tiled=True
        ).astype(jnp.float32),
        lax.psum_scatter(
            grad_outw.astype(jnp.bfloat16), "seq", scatter_dimension=0, tiled=True
        ).astype(jnp.float32),
        lax.psum_scatter(
            grad_up.astype(jnp.bfloat16), "seq", scatter_dimension=0, tiled=True
        ).astype(jnp.float32),
        lax.psum_scatter(
            grad_down.astype(jnp.bfloat16), "seq", scatter_dimension=0, tiled=True
        ).astype(jnp.float32),
    )
    shares = (
        lax.psum(shares[0].astype(jnp.bfloat16), "row").astype(jnp.float32),
        lax.psum(shares[1].astype(jnp.bfloat16), "row").astype(jnp.float32),
        lax.psum(shares[2].astype(jnp.bfloat16), "row").astype(jnp.float32),
        lax.psum(shares[3].astype(jnp.bfloat16), "row").astype(jnp.float32),
    )
    return (
        block_out,
        grad_input,
        summed[0],
        summed[1],
        shares[0],
        summed[2],
        summed[3],
        summed[4],
        summed[5],
        summed[6],
        summed[7],
        summed[8],
        summed[9],
        shares[1],
        summed[10],
        summed[11],
        shares[2],
        shares[3],
    )


def solution(mesh):
    placed = (
        P("row", "seq", None),
        P("row", None),
        P(),
        P(),
        P(),
        P(),
        P(),
        P(),
        P(),
        P(),
        P(),
        P(),
        P(),
        P(),
        P(),
        P(),
        P(),
        P(),
        P(),
        P("row", "seq", None),
    )
    return jax.shard_map(
        shards,
        mesh=mesh,
        in_specs=placed,
        out_specs=(
            P("row", "seq", None),
            P("row", "seq", None),
            P(),
            P(),
            P("seq", None),
            P(),
            P(),
            P(),
            P(),
            P(),
            P(),
            P(),
            P(),
            P("seq", None),
            P(),
            P(),
            P("seq", None),
            P("seq", None),
        ),
        check_vma=False,
    )
```

profile of v0, /device:TPU:0, one launch (start us, length us, event | category | flops | bytes accessed | tf_op | source)
XLA Modules:
  0.0 1079.0 jit_solution(10625518509667225604)
XLA Ops:
  16.2 5.4 collective-permute-start
  29.8 5.3 convolution_add_fusion
  62.2 5.4 all-to-all-start
  79.8 7.4 all-to-all-done
  135.2 5.4 copy.113
  140.7 8.8 reshape.371
  149.5 25.4 %all_to_all.48 = bf16[16,2,12288]{2,1,0:T(2,128)(2,1)} all-to-all(bf16[16,2,12288]{2,1,0:T(2,128)(2,1)} %reshape.371), channel_id=1, replica_groups=mesh['row'=2,'seq'=16] {'seq'}, dimensions={0} | all-to-all | bytes 1572864 | tf_op jit(solution)/shard_map/all_to_all | solution.py:187
  174.9 9.2 reshape.372
  184.1 5.4 copy.114
  199.7 5.4 fusion.14
  205.2 6.1 fusion.6
  220.1 8.4 bitcast_convert_fusion
  240.6 7.5 bitcast_convert_fusion.1
  248.1 12.6 %all-to-all-done.2 = bf16[2,768,256]{2,0,1:T(2,128)(2,1)} async-done(((bf16[2,768,256]{2,0,1:T(2,128)(2,1)}), bf16[2,768,256]{2,0,1:T(2,128)(2,1)}, u32[]{:S(2)}, u32[]{:S(2)}) %all-to-all-start.2) | async-done | bytes 786464 | tf_op jit(solution)/shard_map/all_to_all | solution.py:230
  280.1 6.2 subtract_reduce_fusion
  313.7 5.4 copy.122
  319.1 9.0 reshape.373
  328.1 26.7 %all_to_all.49 = bf16[16,2,12288]{2,1,0:T(2,128)(2,1)} all-to-all(bf16[16,2,12288]{2,1,0:T(2,128)(2,1)} %reshape.373), channel_id=1, replica_groups=mesh['row'=2,'seq'=16] {'seq'}, dimensions={0} | all-to-all | bytes 1572864 | tf_op jit(solution)/shard_map/all_to_all | solution.py:249
  354.8 9.2 reshape.374
  364.0 5.4 copy.123
  382.5 5.2 multiply_reduce_fusion.2
  398.1 6.7 bitcast_convert_fusion.2
  405.1 9.5 add_convert_fusion.1
  424.7 5.3 fusion.92
  430.0 6.8 convolution_multiply_fusion.1
  436.8 51.9 %reduce-scatter.11.cloned.1.call-done = bf16[192,768]{1,0:T(8,128)(2,1)} async-done(((bf16[3072,768]{1,0:T(8,128)(2,1)}), bf16[192,768]{1,0:T(8,128)(2,1)}) %reduce-scatter.11.cloned.1.call-update) | async-done | bytes 294928 | tf_op jit(solution)/shard_map/reduce_scatter | solution.py:310
  488.7 142.6 %reduce-scatter.9.cloned.1.call-done = bf16[48,3072]{1,0:T(8,128)(2,1)} async-done(((bf16[768,3072]{1,0:T(8,128)(2,1)}), bf16[48,3072]{1,0:T(8,128)(2,1)}) %reduce-scatter.9.cloned.1.call-update) | async-done | bytes 294928 | tf_op jit(solution)/shard_map/reduce_scatter | solution.py:307
  631.4 138.3 %reduce-scatter.5.cloned.1.call-done = bf16[48,2304]{1,0:T(8,128)(2,1)} async-done(((bf16[768,2304]{1,0:T(8,128)(2,1)}), bf16[48,2304]{1,0:T(8,128)(2,1)}) %reduce-scatter.5.cloned.1.call-update) | async-done | bytes 221200 | tf_op jit(solution)/shard_map/reduce_scatter | solution.py:301
  776.3 7.5 multiply_reduce_fusion.7
  794.8 5.5 fusion.402
  813.5 107.4 %all-reduce.10.cloned.1.call-done = f32[64,768]{1,0:T(8,128)} async-done(((f32[64,768]{1,0:T(8,128)}), f32[64,768]{1,0:T(8,128)}) %all-reduce.10.cloned.1.call-update) | async-done | bytes 196624 | tf_op jit(solution)/shard_map/psum | solution.py:283
  920.9 135.6 %all-reduce.12.cloned.1.call-done = (f32[768]{0:T(1024)}, f32[768]{0:T(1024)}, f32[3,2304]{1,0:T(4,128)}, f32[33,64]{1,0:T(8,128)}, f32[64]{0:T(128)}, /*index=5...) async-done(((f32[768]{0:T(1024)}, f32[768]{0:T(1024)}, f32[3,2304]{1,0:T(4,128)}, f32[33,64]{1,0:T(8,128)}, ...) | async-done | bytes 68624 | tf_op jit(solution)/shard_map/psum | solution.py:283
  (349 shorter events, 261.2 us)
Async XLA Ops:
  16.2 35.2 %collective-permute-start = (bf16[2,2304,2]{1,2,0:T(2,128)(2,1)}, bf16[2,2304,2]{1,2,0:T(2,128)(2,1)}, u32[]{:S(2)}, u32[]{:S(2)}) collective-permute-start(bf16[2,2304,2]{1,2,0:T(2,128)(2,1)} %slice.85), channel_id=1, source_target_pairs={{0,1},{1,2},{2,3},{3,4},{4,5},{5,6},{6,7},{7,8},{8,9},{9,10},{10,1... | collective-permute-start | bytes 55304 | tf_op jit(solution)/shard_map/ppermute | solution.py:14
  23.8 17.6 %copy-start.48 = (f32[4096,1]{0,1:T(1,128)}, f32[4096,1]{0,1:T(1,128)S(1)}, u32[]{:S(2)}) copy-start(f32[4096,1]{0,1:T(1,128)S(1)} %convert_multiply_fusion.1) | copy-start | bytes 49156
  27.0 9.1 copy-start.61
  29.8 11.4 %copy-start.23 = (f32[4096,64]{0,1:T(8,128)}, f32[4096,64]{0,1:T(8,128)S(1)}, u32[]{:S(2)}) copy-start(f32[4096,64]{0,1:T(8,128)S(1)} %convolution_add_fusion.1) | copy-start | bytes 3145732
  62.2 24.9 %all-to-all-start = ((bf16[2,768,256]{2,0,1:T(2,128)(2,1)}), bf16[2,768,256]{2,0,1:T(2,128)(2,1)}, u32[]{:S(2)}, u32[]{:S(2)}) async-start(bf16[2,768,256]{2,0,1:T(2,128)(2,1)} %copy.109), calls=%async_computation | async-start | bytes 1572864 | tf_op jit(solution)/shard_map/all_to_all | solution.py:168
  67.6 369.2 %reduce-scatter.7.cloned.1.call-start = ((), (), s32[]{:S(2)}) async-start(), calls=%async_computation.10 | async-start | bytes 1253376 | tf_op jit(solution)/shard_map/reduce_scatter | solution.py:304
  67.8 9.1 copy-start.15
  67.8 9.1 copy-start.19
  68.8 63.5 %copy-start.82 = (f32[48]{0:T(128)}, f32[48]{0:T(128)S(1)}, u32[]{:S(2)}) copy-start(f32[48]{0:T(128)S(1)} %dynamic_slice.11) | copy-start | bytes 580
  106.8 13.8 %copy-start.6 = (f32[2,48,64,128]{3,2,1,0:T(8,128)}, f32[2,48,64,128]{3,2,1,0:T(8,128)S(1)}, u32[]{:S(2)}) copy-start(f32[2,48,64,128]{3,2,1,0:T(8,128)S(1)} %convolution_subtract_fusion.3) | copy-start | bytes 9437188
  110.3 10.4 copy-start.8
  199.3 15.5 %copy-start.40 = (f32[2,256,768]{2,1,0:T(8,128)}, f32[2,256,768]{2,1,0:T(8,128)S(1)}, u32[]{:S(2)}) copy-start(f32[2,256,768]{2,1,0:T(8,128)S(1)} %get-tuple-element.70) | copy-start | bytes 4718596
  199.7 11.6 %slice-start.2 = ((s8[4718592]{0:T(1024)(128)(4,1)}), s8[4194304]{0:T(1024)(128)(4,1)S(1)}, s32[]{:S(2)}) async-start(s8[4718592]{0:T(1024)(128)(4,1)} %bitcast.322), calls=%async_computation.17 | async-start | bytes 8388608
  219.6 269.1 %reduce-scatter.11.cloned.1.call-start = ((), (), s32[]{:S(2)}) async-start(), calls=%async_computation.12 | async-start | bytes 5013504 | tf_op jit(solution)/shard_map/reduce_scatter | solution.py:310
  236.2 24.5 %all-to-all-start.2 = ((bf16[2,768,256]{2,0,1:T(2,128)(2,1)}), bf16[2,768,256]{2,0,1:T(2,128)(2,1)}, u32[]{:S(2)}, u32[]{:S(2)}) async-start(bf16[2,768,256]{2,0,1:T(2,128)(2,1)} %copy.118), calls=%async_computation.2 | async-start | bytes 1572864 | tf_op jit(solution)/shard_map/all_to_all | solution.py:230
  240.5 390.9 %reduce-scatter.9.cloned.1.call-start = ((), (), s32[]{:S(2)}) async-start(), calls=%async_computation.11 | async-start | bytes 5013504 | tf_op jit(solution)/shard_map/reduce_scatter | solution.py:307
  248.0 521.6 %reduce-scatter.5.cloned.1.call-start = ((), (), s32[]{:S(2)}) async-start(), calls=%async_computation.8 | async-start | bytes 3760128 | tf_op jit(solution)/shard_map/reduce_scatter | solution.py:301
  387.7 10.4 copy-start.59
  387.7 10.4 copy-start.65
  387.7 10.4 copy-start.75
  387.7 10.4 copy-start.86
  391.8 5.7 collective-permute-start.1
  404.8 401.7 %all-reduce.14.cloned.1.call-start = ((), (), s32[]{:S(2)}) async-start(), calls=%async_computation.14 | async-start | bytes 1769472 | tf_op jit(solution)/shard_map/psum | solution.py:315
  405.1 9.5 copy-start.25
  769.7 14.1 %copy-start.49 = (f32[4096,1]{0,1:T(1,128)S(1)}, f32[4096,1]{0,1:T(1,128)}, u32[]{:S(2)}) copy-start(f32[4096,1]{0,1:T(1,128)} %copy-done.48) | copy-start | bytes 49156
  769.7 151.2 %all-reduce.10.cloned.1.call-start = ((), (), s32[]{:S(2)}) async-start(), calls=%async_computation.9 | async-start | bytes 393216 | tf_op jit(solution)/shard_map/psum | solution.py:283
  776.2 7.5 copy-start.45
  776.2 7.5 copy-start.46
  776.2 7.5 copy-start.63
  776.2 9.2 copy-start.24
  776.3 9.2 copy-start.36
  790.6 265.9 %all-reduce.12.cloned.1.call-start = ((), (), s32[]{:S(2)}) async-start(), calls=%async_computation.13 | async-start | bytes 224256 | tf_op jit(solution)/shard_map/psum | solution.py:283
  (74 other events, 239.8 us)
Sparse Core Ops, SparseCore 0:
  219.8 127.3 reduce-scatter.6
  352.3 136.3 reduce-scatter.10
  494.7 136.5 reduce-scatter.8
  636.3 133.2 reduce-scatter.4
  772.1 18.5 all-reduce.13
  796.7 124.1 all-reduce.9
  928.5 127.9 all-reduce.11
where the time goes:
time: 1090 us; the launch traced here: 1080 us
  waiting for transfers between devices  600 us (55%)
  matrix products  203 us (19%)
  local copies, waits for them, and re-layouts  133 us (12%)
  other arithmetic  57.6 us (5%)
  blocking collectives  52.1 us (5%)
  starting transfers between devices  17.7 us (2%)
  between operations  15.9 us (1%)
    psum x2, waiting for transfers between devices, shards(): lax.psum((grad_mixer_gain, grad_mixer_bias, grad_taps, grad_first_w, grad...  243 us
    reduce_scatter x1, waiting for transfers between devices, shards(): lax.psum_scatter(grad_up.astype(jnp.bfloat16), 'seq', scatter_dimension=0...  143 us
    reduce_scatter x1, waiting for transfers between devices, shards(): lax.psum_scatter(grad_inw.astype(jnp.bfloat16), 'seq', scatter_dimension=...  138 us
    unnamed x209, local copies, waits for them, and re-layouts  67.7 us
    reduce_scatter x1, waiting for transfers between devices, shards(): lax.psum_scatter(grad_down.astype(jnp.bfloat16), 'seq', scatter_dimension...  51.9 us
    all_to_all x1, blocking collectives, shards(): lax.all_to_all(grad_signal.astype(jnp.bfloat16), 'seq', split_axis=2, con...  26.7 us
    all_to_all x1, blocking collectives, shards(): lax.all_to_all(conv.astype(jnp.bfloat16), 'seq', split_axis=2, concat_axi...  25.4 us
  transfers between devices with their start and end apart: 11, of which 8 were waited for; matrix products, arithmetic and copies ran while one was open for 23% of the time, Pallas kernels for 0%

commit v1 on v0

--- a/solution.py
+++ b/solution.py
@@ -1,8 +1,11 @@
+import functools
 import math
 
 import jax
 import jax.numpy as jnp
 from jax import lax
+from jax.experimental import pallas as pl
+from jax.experimental.pallas import tpu as pltpu
 from jax.sharding import PartitionSpec as P
 
 HIGHEST = lax.Precision.HIGHEST
@@ -105,6 +108,377 @@
     ) - jnp.einsum("kn,...km->...nm", first_table[1], turn_imag, precision=HIGHEST)
     grid_view = grid_view * (1.0 / (2 * half_rows * col_count))
     return grid_view.reshape(leading + (half_rows * col_count,))
+
+
+MESH = pl.DeviceIdType.MESH
+VMEM_LIMIT = 56 * 1024 * 1024
+
+
+def seq_weights(core, groups):
+    weights = []
+    w = 1
+    while w < groups:
+        weights.append(w)
+        w *= 2
+    first = weights[0] + core * (weights[1] - weights[0])
+    second = weights[1] - core * (weights[1] - weights[0])
+    return [first, second] + weights[2:]
+
+
+def reduce_kernel(
+    rows,
+    groups,
+    gin,
+    gout,
+    gup,
+    gdown,
+    small,
+    last,
+    in_o,
+    out_o,
+    up_o,
+    down_o,
+    small_o,
+    last_o,
+    own,
+    core_buf,
+    step_buf,
+    wide_buf,
+    fin_own,
+    fin_buf,
+    small_row,
+    small_sum,
+    small_part,
+    small_done,
+    last_row,
+    last_sum,
+    core_ss,
+    core_rs,
+    step_ss,
+    step_rs,
+    wide_ss,
+    wide_rs,
+    fin_sem,
+    srow_ss,
+    srow_rs,
+    spart_ss,
+    spart_rs,
+    sdone_ss,
+    sdone_rs,
+    lrow_ss,
+    lrow_rs,
+    last_ss,
+    last_rs,
+):
+    me = lax.axis_index("seq")
+    row = lax.axis_index("row")
+    core = lax.rem(row, 2)
+    sib = row + 1 - 2 * core
+    unit_rows, half = own.shape[2], own.shape[3]
+    chunk = small_part.shape[1]
+    barrier = pltpu.get_barrier_semaphore()
+    for d in range(1, rows):
+        pl.semaphore_signal(
+            barrier, inc=1, device_id={"row": lax.rem(row + d, rows)}, device_id_type=MESH
+        )
+    for d in range(1, groups):
+        pl.semaphore_signal(
+            barrier, inc=1, device_id={"seq": lax.rem(me + d, groups)}, device_id_type=MESH
+        )
+    pl.semaphore_wait(barrier, rows + groups - 2)
+
+    weights = seq_weights(core, groups)
+    bits = [lax.rem(me // w, 2) for w in weights]
+    steps = len(weights)
+    sib_weights = seq_weights(1 - core, groups)
+    sib_bits = [lax.rem(me // w, 2) for w in sib_weights]
+
+    def shard_of(k, i, mine, weights=weights, bits=bits):
+        at = 0
+        for j in range(k):
+            at = at + bits[j] * weights[j]
+        at = at + (bits[k] if mine else 1 - bits[k]) * weights[k]
+        for j in range(k + 1, steps):
+            t = (i >> (steps - 1 - j)) & 1
+            at = at + (bits[j] if t else 1 - bits[j]) * weights[j]
+        return at
+
+    order = [(False, i) for i in range(groups // 2)] + [(True, i) for i in range(groups // 2)]
+    sib_order = [shard_of(0, i, mine, sib_weights, sib_bits) for mine, i in order]
+    order = [shard_of(0, i, mine) for mine, i in order]
+    parts = [(gin, 3, unit_rows, 0), (gout, 1, unit_rows, 3), (gup, 4, unit_rows, 4)]
+
+    def core_copies(n, s):
+        out = []
+        for p, (ref, cols, _, _) in enumerate(parts):
+            out.append(
+                (ref.at[pl.ds(s * unit_rows, unit_rows), pl.ds((1 - core) * cols * half, cols * half)], p)
+            )
+        out.append((gdown.at[pl.ds(s * 4 * unit_rows, 4 * unit_rows), pl.ds((1 - core) * half, half)], 3))
+        dst = [
+            core_buf[0].at[n],
+            core_buf[1].at[n],
+            core_buf[2].at[n],
+            core_buf[3].at[n],
+        ]
+        return [
+            pltpu.make_async_remote_copy(
+                src_ref=src,
+                dst_ref=dst[p],
+                send_sem=core_ss.at[n, p],
+                recv_sem=core_rs.at[n, p],
+                device_id={"row": sib},
+                device_id_type=MESH,
+            )
+            for src, p in out
+        ]
+
+    srow = [
+        pltpu.make_async_remote_copy(
+            src_ref=small,
+            dst_ref=small_row.at[d - 1],
+            send_sem=srow_ss.at[d - 1],
+            recv_sem=srow_rs.at[d - 1],
+            device_id={"row": lax.rem(row + d, rows)},
+            device_id_type=MESH,
+        )
+        for d in range(1, rows)
+    ]
+    lrow = [
+        pltpu.make_async_remote_copy(
+            src_ref=last,
+            dst_ref=last_row.at[d - 1],
+            send_sem=lrow_ss.at[d - 1],
+            recv_sem=lrow_rs.at[d - 1],
+            device_id={"row": lax.rem(row + d, rows)},
+            device_id_type=MESH,
+        )
+        for d in range(1, rows)
+    ]
+    for c in srow + lrow:
+        c.start()
+    core_list = [core_copies(n, s) for n, s in enumerate(sib_order)]
+    for cs in core_list:
+        for c in cs:
+            c.start()
+
+    for c in srow + lrow:
+        c.wait()
+    total = small[...]
+    tail = last[...]
+    for d in range(rows - 1):
+        total = total + small_row[d]
+        tail = tail + last_row[d]
+    small_sum[...] = total
+    last_sum[...] = tail
+    last_o[me] = tail
+    spart = []
+    lcp = []
+    for d in range(1, groups):
+        to = lax.rem(me + d, groups)
+        spart.append(
+            pltpu.make_async_remote_copy(
+                src_ref=small_sum.at[pl.ds(to * chunk, chunk)],
+                dst_ref=small_part.at[d - 1],
+                send_sem=spart_ss.at[d - 1],
+                recv_sem=spart_rs.at[d - 1],
+                device_id={"seq": to},
+                device_id_type=MESH,
+            )
+        )
+        lcp.append(
+            pltpu.make_async_remote_copy(
+                src_ref=last_sum,
+                dst_ref=last_o.at[me],
+                send_sem=last_ss.at[d - 1],
+                recv_sem=last_rs.at[d - 1],
+                device_id={"seq": to},
+                device_id_type=MESH,
+            )
+        )
+    for c in spart + lcp:
+        c.start()
+
+    def step_copy(k, i):
+        return pltpu.make_async_remote_copy(
+            src_ref=own.at[shard_of(k, i, False)],
+            dst_ref=step_buf[k].at[i],
+            send_sem=step_ss[k].at[i],
+            recv_sem=step_rs[k].at[i],
+            device_id={"seq": me + weights[k] * (1 - 2 * bits[k])},
+            device_id_type=MESH,
+        )
+
+    def add_core(n, s):
+        for ref, cols, _, first in parts:
+            buf = core_buf[{0: 0, 3: 1, 4: 2}[first]]
+            for c in range(cols):
+                mine = ref[
+                    pl.ds(s * unit_rows, unit_rows), pl.ds(core * cols * half + c * half, half)
+                ]
+                own[s, first + c] = mine + buf[n, :, c * half : (c + 1) * half]
+        for c in range(4):
+            mine = gdown[
+                pl.ds(s * 4 * unit_rows + c * unit_rows, unit_rows), pl.ds(core * half, half)
+            ]
+            own[s, 8 + c] = mine + core_buf[3][n, c * unit_rows : (c + 1) * unit_rows]
+
+    copies = [[step_copy(k, i) for i in range(groups >> (k + 1))] for k in range(steps)]
+    for n, s in enumerate(order):
+        for c in core_list[n]:
+            c.wait_recv()
+        add_core(n, s)
+        if n < groups // 2:
+            copies[0][n].start()
+
+    for c in spart:
+        c.wait()
+    total = small_sum[pl.ds(me * chunk, chunk)]
+    for d in range(groups - 1):
+        total = total + small_part[d]
+    small_done[...] = total
+    small_o[pl.ds(me * chunk, chunk)] = total
+    sdone = [
+        pltpu.make_async_remote_copy(
+            src_ref=small_done,
+            dst_ref=small_o.at[pl.ds(me * chunk, chunk)],
+            send_sem=sdone_ss.at[d - 1],
+            recv_sem=sdone_rs.at[d - 1],
+            device_id={"seq": lax.rem(me + d, groups)},
+            device_id_type=MESH,
+        )
+        for d in range(1, groups)
+    ]
+    for c in sdone:
+        c.start()
+
+    for k in range(steps):
+        count = groups >> (k + 1)
+        for i in range(count):
+            copies[k][i].wait_recv()
+            s = shard_of(k, i, True)
+            own[s] = own[s] + step_buf[k][i]
+            if k + 1 < steps and i < count // 2:
+                copies[k + 1][i].start()
+
+    w = 2
+    n = 0
+    while w < rows:
+        bit = lax.rem(row // w, 2)
+        c = pltpu.make_async_remote_copy(
+            src_ref=own.at[me],
+            dst_ref=wide_buf.at[n],
+            send_sem=wide_ss.at[n],
+            recv_sem=wide_rs.at[n],
+            device_id={"row": row + w * (1 - 2 * bit)},
+            device_id_type=MESH,
+        )
+        c.start()
+        c.wait()
+        own[me] = own[me] + wide_buf[n]
+        w *= 2
+        n += 1
+
+    fin_own[...] = own[me]
+    fin = pltpu.make_async_remote_copy(
+        src_ref=fin_own,
+        dst_ref=fin_buf,
+        send_sem=fin_sem.at[0],
+        recv_sem=fin_sem.at[1],
+        device_id={"row": sib},
+        device_id_type=MESH,
+    )
+    fin.start()
+
+    def put(where, buf):
+        for ref, cols, _, first in parts:
+            out = {0: in_o, 3: out_o, 4: up_o}[first]
+            for c in range(cols):
+                out[:, pl.ds(where * cols * half + c * half, half)] = buf[first + c].astype(
+                    jnp.float32
+                )
+        for c in range(4):
+            down_o[c * unit_rows : (c + 1) * unit_rows, pl.ds(where * half, half)] = buf[
+                8 + c
+            ].astype(jnp.float32)
+
+    put(core, fin_own)
+    for cs in core_list:
+        for c in cs:
+            c.wait_send()
+    for cs in copies:
+        for c in cs:
+            c.wait_send()
+    for c in sdone + lcp:
+        c.wait()
+    fin.wait()
+    put(1 - core, fin_buf)
+
+
+def reduce_all(gin, gout, gup, gdown, small, last):
+    rows, groups = lax.axis_size("row"), lax.axis_size("seq")
+    width = gin.shape[0]
+    unit = width // groups
+    half = width // 2
+    wide = max(1, rows.bit_length() - 2)
+    low, f32 = jnp.bfloat16, jnp.float32
+    steps = groups.bit_length() - 1
+    chunk = small.shape[0] // groups
+    dma = pltpu.SemaphoreType.DMA
+    vm = pl.BlockSpec(memory_space=pltpu.VMEM)
+    return pl.pallas_call(
+        functools.partial(reduce_kernel, rows, groups),
+        out_shape=(
+            jax.ShapeDtypeStruct((unit, 3 * width), f32),
+            jax.ShapeDtypeStruct((unit, width), f32),
+            jax.ShapeDtypeStruct((unit, 4 * width), f32),
+            jax.ShapeDtypeStruct((4 * unit, width), f32),
+            jax.ShapeDtypeStruct(small.shape, f32),
+            jax.ShapeDtypeStruct((groups,) + last.shape, f32),
+        ),
+        in_specs=[vm] * 6,
+        out_specs=(vm,) * 6,
+        scratch_shapes=[
+            pltpu.VMEM((groups, 12, unit, half), low),
+            [
+                pltpu.VMEM((groups, unit, 3 * half), low),
+                pltpu.VMEM((groups, unit, half), low),
+                pltpu.VMEM((groups, unit, 4 * half), low),
+                pltpu.VMEM((groups, 4 * unit, half), low),
+            ],
+            [pltpu.VMEM((groups >> (k + 1), 12, unit, half), low) for k in range(steps)],
+            pltpu.VMEM((wide, 12, unit, half), low),
+            pltpu.VMEM((12, unit, half), low),
+            pltpu.VMEM((12, unit, half), low),
+            pltpu.VMEM((rows - 1,) + small.shape, f32),
+            pltpu.VMEM(small.shape, f32),
+            pltpu.VMEM((groups - 1, chunk, small.shape[1]), f32),
+            pltpu.VMEM((chunk, small.shape[1]), f32),
+            pltpu.VMEM((rows - 1,) + last.shape, f32),
+            pltpu.VMEM(last.shape, f32),
+            dma((groups, 4)),
+            dma((groups, 4)),
+            [dma((groups >> (k + 1),)) for k in range(steps)],
+            [dma((groups >> (k + 1),)) for k in range(steps)],
+            dma((wide,)),
+            dma((wide,)),
+            dma((2,)),
+            dma((rows - 1,)),
+            dma((rows - 1,)),
+            dma((groups - 1,)),
+            dma((groups - 1,)),
+            dma((groups - 1,)),
+            dma((groups - 1,)),
+            dma((rows - 1,)),
+            dma((rows - 1,)),
+            dma((groups - 1,)),
+            dma((groups - 1,)),
+        ],
+        compiler_params=pltpu.CompilerParams(
+            collective_id=0, has_side_effects=True, vmem_limit_bytes=VMEM_LIMIT
+        ),
+        name="reduce_all",
+    )(gin, gout, gup, gdown, small, last)
 
 
 def shards(
@@ -274,49 +648,43 @@
     )
     grad_input_part, grad_mixer_gain, grad_mixer_bias = norm_pull(grad_normed)
     grad_input = grad_mixed + grad_input_part
-    grad_last = lax.dynamic_update_slice_in_dim(
-        jnp.zeros(filter_out.shape, jnp.float32), grad_last_part, chan_start, 1
-    )
     grad_skip = lax.dynamic_update_slice_in_dim(
         jnp.zeros(filter_skip.shape, jnp.float32), grad_skip_part, chan_start, 0
     )
-    summed = lax.psum(
-        (
-            grad_mixer_gain,
-            grad_mixer_bias,
-            grad_taps,
-            grad_first_w,
-            grad_first_b,
-            grad_mid_w,
-            grad_mid_b,
-            grad_freq_w,
-            grad_last,
-            grad_skip,
-            grad_feed_gain,
-            grad_feed_bias,
-        ),
-        ("row", "seq"),
-    )
-    shares = (
-        lax.psum_scatter(
-            grad_inw.astype(jnp.bfloat16), "seq", scatter_dimension=0, tiled=True
-        ).astype(jnp.float32),
-        lax.psum_scatter(
-            grad_outw.astype(jnp.bfloat16), "seq", scatter_dimension=0, tiled=True
-        ).astype(jnp.float32),
-        lax.psum_scatter(
-            grad_up.astype(jnp.bfloat16), "seq", scatter_dimension=0, tiled=True
-        ).astype(jnp.float32),
-        lax.psum_scatter(
-            grad_down.astype(jnp.bfloat16), "seq", scatter_dimension=0, tiled=True
-        ).astype(jnp.float32),
-    )
-    shares = (
-        lax.psum(shares[0].astype(jnp.bfloat16), "row").astype(jnp.float32),
-        lax.psum(shares[1].astype(jnp.bfloat16), "row").astype(jnp.float32),
-        lax.psum(shares[2].astype(jnp.bfloat16), "row").astype(jnp.float32),
-        lax.psum(shares[3].astype(jnp.bfloat16), "row").astype(jnp.float32),
-    )
+    pieces = (
+        grad_mixer_gain,
+        grad_mixer_bias,
+        grad_taps,
+        grad_first_w,
+        grad_first_b,
+        grad_mid_w,
+        grad_mid_b,
+        grad_freq_w,
+        grad_skip,
+        grad_feed_gain,
+        grad_feed_bias,
+    )
+    flat = jnp.concatenate([p.reshape(-1) for p in pieces])
+    chunk = -(-flat.shape[0] // (groups * 8 * 128)) * 8
+    flat = jnp.pad(flat, (0, groups * chunk * 128 - flat.shape[0])).reshape(groups * chunk, 128)
+    low = jnp.bfloat16
+    s_in, s_out, s_up, s_down, flat, last_all = reduce_all(
+        grad_inw.astype(low),
+        grad_outw.astype(low),
+        grad_up.astype(low),
+        grad_down.astype(low),
+        flat,
+        grad_last_part,
+    )
+    shares = (s_in, s_out, s_up, s_down)
+    flat = flat.reshape(-1)
+    summed = []
+    at = 0
+    for p in pieces:
+        summed.append(flat[at : at + p.size].reshape(p.shape))
+        at += p.size
+    grad_last = last_all.transpose(1, 0, 2).reshape(filter_out.shape)
+    summed = summed[:8] + [grad_last] + summed[8:]
     return (
         block_out,
         grad_input,

time: 1090 us -> 574 us (0.53)
  waiting for transfers between devices: 600 us -> 12.1 us
  Pallas kernels: 0 us -> 117 us
  blocking collectives: 52.1 us -> 25.4 us
  between operations: 15.9 us -> 2.6 us
    reduce_scatter x4 -> x0, waiting for transfers between devices: 333 us -> none  [the longest x1 143 us: shards(): lax.psum_scatter(grad_up.astype(jnp.bfloat16), 'seq', scatter_dimension=0...]
    psum x3 -> x0, waiting for transfers between devices: 243 us -> none  [the longest x2 243 us: shards(): lax.psum((grad_mixer_gain, grad_mixer_bias, grad_taps, grad_first_w, grad...]
    pallas_call x0 -> x1, Pallas kernels: none -> 117 us  [reduce_all(): pl.pallas_call(functools.partial(reduce_kernel, rows, groups), out_shape=...]
    all_to_all x1 -> x0, blocking collectives: 26.7 us -> none  [shards(): lax.all_to_all(grad_signal.astype(jnp.bfloat16), 'seq', split_axis=2, con...]
    unnamed x209 -> x187, local copies, waits for them, and re-layouts: 67.7 us -> 53.5 us
  transfers between devices with their start and end apart: 11 -> 5, of which waited for: 8 -> 3; matrix products, arithmetic and copies ran while one was open for 23% -> 16% of each run, Pallas kernels for 0% -> 0%
where the time goes in v1:
time: 574 us; the launch traced here: 568 us
  matrix products  201 us (35%)
  local copies, waits for them, and re-layouts  134 us (23%)
  Pallas kernels  117 us (20%)
  other arithmetic  54.3 us (9%)
  blocking collectives  25.4 us (4%)
  starting transfers between devices  21.3 us (4%)
  waiting for transfers between devices  12.1 us (2%)
    pallas_call x1, Pallas kernels, reduce_all(): pl.pallas_call(functools.partial(reduce_kernel, rows, groups), out_shape=...  117 us
    unnamed x187, local copies, waits for them, and re-layouts  53.5 us
    all_to_all x1, blocking collectives, shards(): lax.all_to_all(conv.astype(jnp.bfloat16), 'seq', split_axis=2, concat_axi...  25.4 us
    dot_general x3, matrix products, filter_rows(): jnp.dot(hidden, filter_mid, precision=HIGHEST) + filter_mid_bias  18.5 us
    dot_general x3, matrix products, filter_rows(): raw_filter = jnp.einsum('lh,hc->cl', hidden, out_part, precision=HIGHEST)  18 us
    dot_general x3, matrix products, forward_dft(): jnp.einsum('...kn,nj->...kj', turn_imag, second[1], precision=HIGHEST)  13 us
  transfers between devices with their start and end apart: 5, of which 3 were waited for; matrix products, arithmetic and copies ran while one was open for 16% of the time, Pallas kernels for 0%

profile of v1, /device:TPU:0, one launch (start us, length us, event | category | flops | bytes accessed | tf_op | source)
XLA Modules:
  0.0 567.5 jit_solution(5387249417892829177)
XLA Ops:
  9.6 5.4 collective-permute-start
  22.9 5.3 convolution_add_fusion
  29.2 5.1 fusion.85
  55.6 5.4 all-to-all-start
  73.1 7.4 %all-to-all-done = bf16[2,768,256]{2,0,1:T(2,128)(2,1)} async-done(((bf16[2,768,256]{2,0,1:T(2,128)(2,1)}), bf16[2,768,256]{2,0,1:T(2,128)(2,1)}, u32[]{:S(2)}, u32[]{:S(2)}) %all-to-all-start) | async-done | bytes 786464 | tf_op jit(solution)/shard_map/all_to_all | solution.py:542
  128.6 5.4 copy.116
  134.1 8.8 %reshape.415 = bf16[16,2,12288]{2,1,0:T(2,128)(2,1)} reshape(bf16[4096,2,48]{2,1,0:T(2,128)(2,1)} %bitcast.306) | data formatting | bytes 1572864
  142.9 25.4 %all_to_all.48 = bf16[16,2,12288]{2,1,0:T(2,128)(2,1)} all-to-all(bf16[16,2,12288]{2,1,0:T(2,128)(2,1)} %reshape.415), channel_id=1, replica_groups=mesh['row'=2,'seq'=16] {'seq'}, dimensions={0} | all-to-all | bytes 1572864 | tf_op jit(solution)/shard_map/all_to_all | solution.py:561
  168.3 9.2 %reshape.416 = bf16[4096,2,48]{2,1,0:T(2,128)(2,1)} reshape(bf16[16,2,12288]{2,1,0:T(2,128)(2,1)} %all_to_all.48) | data formatting | bytes 1572864
  177.5 5.4 copy.117
  193.1 4.9 fusion.14
  198.1 4.9 bitcast_convert_fusion.gdown
  203.4 6.3 %fusion.6 = bf16[2,256,3072]{2,1,0:T(8,128)(2,1)S(1)} fusion(f32[2,256,3072]{2,1,0:T(8,128)S(1)} %fusion.14, bf16[2,256,768]{2,1,0:T(8,128)(2,1)S(1)} %copy-done.37, bf16[3072,768]{1,0:T(8,128)(2,1)S(1)} %bitcast.339), kind=kOutput, calls=%fused_computation.11 | convolution fusion | flops 2447376384 | bytes 14942208 | tf_op jit(solution)/shard_map/rtd,fd->rtf/dot_general | solution.py:582
  223.2 4.3 all-to-all-start.2
  227.5 7.6 %bitcast_convert_fusion.1.gup = bf16[768,3072]{1,0:T(8,128)(2,1)} fusion(bf16[2,256,3072]{2,1,0:T(8,128)(2,1)} %copy-done.83, f32[2,256,768]{2,1,0:T(8,128)} %copy-done.35, f32[768]{0:T(1024)} %param.36, f32[768]{0:T(1024)S(1)} %copy-done.78, f32[2,256]{1,0:T(2,128)S(1)} %fusion.247, f32[2,256]{1,0:T(2,128)S(1)} %broadcast_multiply_fusion), kind=kOutput, calls=%fused_computation.1 | convolution fusion | flops 2420244480 | bytes 9447424 | tf_op jit(solution)/shard_map/rtd,rtf->df/dot_general | solution.py:586
  235.1 8.8 %add_convert_fusion.1 = bf16[2,256,768]{2,1,0:T(8,128)(2,1)} fusion(f32[2,256,768]{2,1,0:T(8,128)S(1)} %copy-done.36, bf16[3072,768]{1,0:T(8,128)(2,1)} %param.38, f32[2,256,3072]{2,1,0:T(8,128)} %copy-done.82), kind=kOutput, calls=%fused_computation.131 | convolution fusion | flops 2430861312 | bytes 13369344 | tf_op jit(solution)/shard_map/rtf,fd->rtd/dot_general | solution.py:578
  259.9 4.6 fusion.105
  267.6 7.0 %subtract_reduce_fusion = (f32[48,64,128]{2,1,0:T(8,128)S(1)}, f32[48,64,128]{2,1,0:T(8,128)S(1)}, f32[2,48,64,128]{3,2,1,0:T(8,128)S(1)}) fusion(f32[2,48,64,128]{3,2,1,0:T(8,128)S(1)} %copy-done.7, f32[2,48,64,128]{3,2,1,0:T(8,128)S(1)} %copy-done.9, f32[2,48,64,128]{3,2,1,0:T(8,128)S(1)} %convolution_subtract_fusion.1, f32[2,48,64,128]{3,2,1,0:T(8,128)} %fusion.105, ...), kind=kOutput, calls=%fused_computation.54 | convolution fusion | flops 1217626112 | bytes 25231360 | tf_op jit(solution)/shard_map/...kn,nj->...kj/dot_general | solution.py:86
  310.4 5.4 copy.125
  315.9 8.8 %reshape.417 = bf16[16,2,12288]{2,1,0:T(2,128)(2,1)} reshape(bf16[4096,2,48]{2,1,0:T(2,128)(2,1)} %bitcast.308) | data formatting | bytes 1572864
  324.7 5.0 all-to-all-start.3
  329.7 6.1 %convolution_multiply_fusion.1 = f32[4096,64]{0,1:T(8,128)S(1)} fusion(f32[4096,64]{0,1:T(8,128)} %copy-done.13, f32[6,8,32,128]{3,2,1,0:T(8,128)} %bitcast.312, f32[64]{0:T(128)S(1)} %copy-done.59, f32[48]{0:T(128)S(1)} %copy-done.76, f32[64,768]{1,0:T(8,128)} %param.31, s32[]{:T(128)S(6)} %select_n.164), kind=kOutput, calls=%fused_computation.30 | convolution fusion | flops 151912448 | bytes 2916804 | tf_op jit(solution)/shard_map/transpose(jvp(lh,hc->cl))/dot_general | solution.py:51
  336.8 5.8 %fusion.91 = f32[64,64]{1,0:T(8,128)} fusion(f32[4096,64]{0,1:T(8,128)S(1)} %copy-done.21, f32[4096,64]{0,1:T(8,128)S(1)} %convolution_multiply_fusion.1, f32[64]{0:T(128)} %param.30), kind=kOutput, calls=%fused_computation.167 | convolution fusion | flops 201850880 | bytes 2113792 | tf_op jit(solution)/shard_map/transpose(jvp())/dot_general | solution.py:49
  344.0 7.4 %multiply_reduce_fusion.7 = (f32[64]{0:T(128)}, f32[64]{0:T(128)}, f32[64]{0:T(128)}, f32[64]{0:T(128)}, f32[4096,64]{0,1:T(8,128)S(1)}) fusion(f32[4096,64]{0,1:T(8,128)} %copy-done.29, f32[4096,64]{0,1:T(8,128)} %copy-done.13, f32[64]{0:T(128)} %param.30, f32[4096,64]{0,1:T(8,128)} %copy-done.20, f32[64,64]{1,0:T(8,128)} %param.28), kind=kOutput, calls=%fused_computation.160 | convolution fusion | flops 204209920 | bytes 4211968 | tf_op jit(solution)/shard_map/transpose(jvp())/dot_general | solution.py:49
  357.8 6.8 %fusion.92.last = f32[64,48]{1,0:T(8,128)} fusion(f32[4096,64]{0,1:T(8,128)} %copy-done.13, f32[6,8,32,128]{3,2,1,0:T(8,128)} %bitcast.313, f32[64]{0:T(128)} %param.30, f32[48]{0:T(128)} %copy-done.75), kind=kOutput, calls=%fused_computation.168 | convolution fusion | flops 151650304 | bytes 1847744 | tf_op jit(solution)/shard_map/transpose(jvp(lh,hc->cl))/dot_general | solution.py:51
  364.6 9.2 %reshape.418 = bf16[4096,2,48]{2,1,0:T(2,128)(2,1)} reshape(bf16[16,2,12288]{2,1,0:T(2,128)(2,1)} %all-to-all-done.3) | data formatting | bytes 1572864
  373.8 5.4 copy.126
  388.7 8.4 %multiply_reduce_fusion.2 = (f32[2304]{0:T(1024)S(1)}, f32[2304]{0:T(1024)S(1)}, f32[2304]{0:T(1024)S(1)}, f32[2,2304,256]{1,2,0:T(8,128)S(1)}, f32[2,2304,256]{1,2,0:T(8,128)S(1)}) fusion(f32[2,2304,258]{1,2,0:T(8,128)} %copy-done.5, f32[256]{0:T(256)S(1)} %copy-done.74, f32[2,768,256]{1,2,0:T(8,128)S(1)} %get-tuple-element.55, ...), kind=kLoop, calls=%fused_computation.27 | loop fusion | flops 15328512 | bytes 28362752 | tf_op jit(solution)/shard_map/reduce_sum | solution.py:635
  408.3 5.4 fusion.402
  418.2 6.7 %bitcast_convert_fusion.2.gin = bf16[768,2304]{1,0:T(8,128)(2,1)} fusion(bf16[2,256,768]{2,1,0:T(8,128)(2,1)} %param.20, f32[768]{0:T(1024)} %param.23, f32[768]{0:T(1024)} %param.22, f32[2,256]{1,0:T(2,128)} %copy-done.62, f32[2,256]{1,0:T(2,128)} %copy-done.56, f32[2,2304,258]{1,2,0:T(8,128)} %pad_add_fusion, bf16[2,2304,2]{1,2,0:T(2,128)(2,1)} %collective-permute-done.1), kind=kOutput, calls=%fused_computation.4 | convolution fusion | flops 1819607040 | bytes 9074688 | tf_op jit(solution)/shard_map/rtd,rct->dc/dot_general | solution.py:643
  424.9 117.0 %reduce_all.1 = (f32[48,2304]{1,0:T(8,128)}, f32[48,768]{1,0:T(8,128)}, f32[48,3072]{1,0:T(8,128)}, f32[192,768]{1,0:T(8,128)}, f32[256,128]{1,0:T(8,128)}, /*index=5*/f32[16,64,48]{2,1,0:T(8,128)}) custom-call(bf16[768,2304]{1,0:T(8,128)(2,1)} %bitcast_convert_fusion.2.gin, bf16[768,768]{1,0:T(8,128)(2,1)} %bitcast_convert_fusion.3.gout, ...), custom_call_target="tpu_custom_call" | custom-call | tf_op jit(solution)/shard_map/reduce_all/pallas_call | solution.py:429
  547.8 4.3 add_add_fusion.2
  (316 shorter events, 232.1 us)
Async XLA Ops:
  9.6 35.1 %collective-permute-start = (bf16[2,2304,2]{1,2,0:T(2,128)(2,1)}, bf16[2,2304,2]{1,2,0:T(2,128)(2,1)}, u32[]{:S(2)}, u32[]{:S(2)}) collective-permute-start(bf16[2,2304,2]{1,2,0:T(2,128)(2,1)} %slice.155), channel_id=1, source_target_pairs={{0,1},{1,2},{2,3},{3,4},{4,5},{5,6},{6,7},{7,8},{8,9},{9,10},{10,1... | collective-permute-start | bytes 55304 | tf_op jit(solution)/shard_map/ppermute | solution.py:17
  17.2 17.2 %copy-start.43 = (f32[4096,1]{0,1:T(1,128)}, f32[4096,1]{0,1:T(1,128)S(1)}, u32[]{:S(2)}) copy-start(f32[4096,1]{0,1:T(1,128)S(1)} %convert_multiply_fusion.1) | copy-start | bytes 49156
  20.1 9.2 %copy-start.58 = (f32[64]{0:T(128)S(1)}, f32[64]{0:T(128)}, u32[]{:S(2)}) copy-start(f32[64]{0:T(128)} %param.30) | copy-start | bytes 772
  20.8 7.4 %copy-start.75 = (f32[48]{0:T(128)}, f32[48]{0:T(128)S(1)}, u32[]{:S(2)}) copy-start(f32[48]{0:T(128)S(1)} %dynamic-slice_negate_fusion) | copy-start | bytes 580
  22.9 11.4 %copy-start.20 = (f32[4096,64]{0,1:T(8,128)}, f32[4096,64]{0,1:T(8,128)S(1)}, u32[]{:S(2)}) copy-start(f32[4096,64]{0,1:T(8,128)S(1)} %convolution_add_fusion.1) | copy-start | bytes 3145732
  43.2 173.3 %copy-start.54 = (f32[2,256]{1,0:T(2,128)}, f32[2,256]{1,0:T(2,128)S(1)}, u32[]{:S(2)}) copy-start(f32[2,256]{1,0:T(2,128)S(1)} %compare_convert_fusion) | copy-start | bytes 6148
  55.6 24.9 %all-to-all-start = ((bf16[2,768,256]{2,0,1:T(2,128)(2,1)}), bf16[2,768,256]{2,0,1:T(2,128)(2,1)}, u32[]{:S(2)}, u32[]{:S(2)}) async-start(bf16[2,768,256]{2,0,1:T(2,128)(2,1)} %copy.112), calls=%async_computation | async-start | bytes 1572864 | tf_op jit(solution)/shard_map/all_to_all | solution.py:542
  61.2 9.1 %copy-start.14 = (f32[64,128]{1,0:T(8,128)}, f32[64,128]{1,0:T(8,128)S(1)}, u32[]{:S(2)}) copy-start(f32[64,128]{1,0:T(8,128)S(1)} %get-tuple-element.84) | copy-start | bytes 98308
  61.2 9.1 %copy-start.17 = (f32[64,128]{1,0:T(8,128)}, f32[64,128]{1,0:T(8,128)S(1)}, u32[]{:S(2)}) copy-start(f32[64,128]{1,0:T(8,128)S(1)} %get-tuple-element.85) | copy-start | bytes 98308
  62.1 63.5 %copy-start.79 = (f32[48]{0:T(128)}, f32[48]{0:T(128)S(1)}, u32[]{:S(2)}) copy-start(f32[48]{0:T(128)S(1)} %dynamic_slice.11) | copy-start | bytes 580
  100.2 13.9 %copy-start.6 = (f32[2,48,64,128]{3,2,1,0:T(8,128)}, f32[2,48,64,128]{3,2,1,0:T(8,128)S(1)}, u32[]{:S(2)}) copy-start(f32[2,48,64,128]{3,2,1,0:T(8,128)S(1)} %convolution_subtract_fusion.3) | copy-start | bytes 9437188
  103.4 10.6 %copy-start.8 = (f32[2,48,64,128]{3,2,1,0:T(8,128)}, f32[2,48,64,128]{3,2,1,0:T(8,128)S(1)}, u32[]{:S(2)}) copy-start(f32[2,48,64,128]{3,2,1,0:T(8,128)S(1)} %convolution_add_fusion.5) | copy-start | bytes 9437188
  192.7 20.5 %copy-start.35 = (f32[2,256,768]{2,1,0:T(8,128)}, f32[2,256,768]{2,1,0:T(8,128)S(1)}, u32[]{:S(2)}) copy-start(f32[2,256,768]{2,1,0:T(8,128)S(1)} %get-tuple-element.75) | copy-start | bytes 4718596
  193.1 10.3 %slice-start.2 = ((s8[4718592]{0:T(1024)(128)(4,1)}), s8[4194304]{0:T(1024)(128)(4,1)S(1)}, s32[]{:S(2)}) async-start(s8[4718592]{0:T(1024)(128)(4,1)} %bitcast.338), calls=%async_computation.6 | async-start | bytes 8388608
  198.1 11.6 %slice-start = ((s8[4718592]{0:T(1024)(128)(4,1)}), s8[4194304]{0:T(1024)(128)(4,1)S(1)}, s32[]{:S(2)}) async-start(s8[4718592]{0:T(1024)(128)(4,1)} %bitcast.336), calls=%async_computation.4 | async-start | bytes 8388608
  223.2 22.7 %all-to-all-start.2 = ((bf16[2,768,256]{2,0,1:T(2,128)(2,1)}), bf16[2,768,256]{2,0,1:T(2,128)(2,1)}, u32[]{:S(2)}, u32[]{:S(2)}) async-start(bf16[2,768,256]{2,0,1:T(2,128)(2,1)} %copy.121), calls=%async_computation.2 | async-start | bytes 1572864 | tf_op jit(solution)/shard_map/all_to_all | solution.py:604
  227.5 7.6 %copy-start.36 = (f32[2,256,768]{2,1,0:T(8,128)S(1)}, f32[2,256,768]{2,1,0:T(8,128)}, u32[]{:S(2)}) copy-start(f32[2,256,768]{2,1,0:T(8,128)} %copy-done.35) | copy-start | bytes 4718596
  310.4 19.3 %copy-start.59 = (f32[64]{0:T(128)S(1)}, f32[64]{0:T(128)}, u32[]{:S(2)}) copy-start(f32[64]{0:T(128)} %param.30) | copy-start | bytes 772
  310.4 19.3 %copy-start.76 = (f32[48]{0:T(128)S(1)}, f32[48]{0:T(128)}, u32[]{:S(2)}) copy-start(f32[48]{0:T(128)} %copy-done.75) | copy-start | bytes 580
  324.7 39.9 %all-to-all-start.3 = ((bf16[16,2,12288]{2,1,0:T(2,128)(2,1)}), bf16[16,2,12288]{2,1,0:T(2,128)(2,1)}, u32[]{:S(2)}, u32[]{:S(2)}) async-start(bf16[16,2,12288]{2,1,0:T(2,128)(2,1)} %reshape.417), calls=%async_computation.3 | async-start | bytes 1572864 | tf_op jit(solution)/shard_map/all_to_all | solution.py:623
  336.8 14.6 %copy-start.44 = (f32[4096,1]{0,1:T(1,128)S(1)}, f32[4096,1]{0,1:T(1,128)}, u32[]{:S(2)}) copy-start(f32[4096,1]{0,1:T(1,128)} %copy-done.43) | copy-start | bytes 49156
  344.0 7.4 %copy-start.40 = (f32[4096,16]{0,1:T(8,128)S(1)}, f32[4096,16]{0,1:T(8,128)}, u32[]{:S(2)}) copy-start(f32[4096,16]{0,1:T(8,128)} %get-tuple-element.73) | copy-start | bytes 786436
  344.0 7.4 %copy-start.60 = (f32[64]{0:T(128)S(1)}, f32[64]{0:T(128)}, u32[]{:S(2)}) copy-start(f32[64]{0:T(128)} %param.30) | copy-start | bytes 772
  356.6 22.5 %copy-start.72 = (f32[768]{0:T(1024)}, f32[768]{0:T(1024)S(1)}, u32[]{:S(2)}) copy-start(f32[768]{0:T(1024)S(1)} %dynamic_update_slice.3) | copy-start | bytes 9220
  388.7 8.5 %copy-start.50 = (f32[2304]{0:T(1024)S(1)}, f32[2304]{0:T(1024)}, u32[]{:S(2)}) copy-start(f32[2304]{0:T(1024)} %copy-done.49) | copy-start | bytes 27652
  402.3 6.0 %collective-permute-start.1 = (bf16[2,2304,2]{1,2,0:T(2,128)(2,1)}, bf16[2,2304,2]{1,2,0:T(2,128)(2,1)}, u32[]{:S(2)}, u32[]{:S(2)}) collective-permute-start(bf16[2,2304,2]{1,2,0:T(2,128)(2,1)} %slice.195), channel_id=1, source_target_pairs={{1,0},{2,1},{3,2},{4,3},{5,4},{6,5},{7,6},{8,7},{9,8},{10,9},{11,1... | collective-permute-start | bytes 55304 | tf_op jit(solution)/shard_map/ppermute | solution.py:17
  405.7 8.0 %copy-start.70 = (f32[2,256]{1,0:T(2,128)S(1)}, f32[2,256]{1,0:T(2,128)}, u32[]{:S(2)}) copy-start(f32[2,256]{1,0:T(2,128)} %copy-done.69) | copy-start | bytes 6148
  405.7 8.1 %copy-start.26 = (bf16[2,256,768]{2,1,0:T(8,128)(2,1)S(1)}, bf16[2,256,768]{2,1,0:T(8,128)(2,1)}, u32[]{:S(2)}) copy-start(bf16[2,256,768]{2,1,0:T(8,128)(2,1)} %param.20) | copy-start | bytes 2359300
  405.7 8.1 %copy-start.57 = (f32[2,256]{1,0:T(2,128)S(1)}, f32[2,256]{1,0:T(2,128)}, u32[]{:S(2)}) copy-start(f32[2,256]{1,0:T(2,128)} %copy-done.56) | copy-start | bytes 6148
  405.7 8.1 %copy-start.63 = (f32[2,256]{1,0:T(2,128)S(1)}, f32[2,256]{1,0:T(2,128)}, u32[]{:S(2)}) copy-start(f32[2,256]{1,0:T(2,128)} %copy-done.62) | copy-start | bytes 6148
  405.7 8.1 %copy-start.71 = (f32[768]{0:T(1024)S(1)}, f32[768]{0:T(1024)}, u32[]{:S(2)}) copy-start(f32[768]{0:T(1024)} %param.22) | copy-start | bytes 9220
  405.7 9.5 %copy-start.53 = (f32[4096]{0:T(1024)S(1)}, f32[4096]{0:T(1024)}, u32[]{:S(2)}) copy-start(f32[4096]{0:T(1024)} %reshape.383) | copy-start | bytes 49156
  (61 other events, 208.7 us)
